TPU v7x, 32 devices: a whole 2x2x4 slice. The times are simulated.
32 devices in a mesh: ax: 8 (over y, x, core), rad: 4 (over z).
Axes of the slice: x: 2, y: 2, z: 4, core: 2. Of those that a mesh axis runs over, the one named last changes fastest.
Arguments:
- couplings: bfloat16 [8, 6, 1728, 1728], P('ax', None, 'rad'), may hold values from -0.071777344 to 0.071777344
- pivots: float32 [8, 1728, 1728], P('ax', 'rad'), may hold values from -0.02946892 to 1.0294689
- pattern: int32 [8, 6, 9, 9], P('ax'), may hold values 0 or 1
- krylov: float32 [8, 32, 1728], P('ax', None, 'rad'), may hold values from -6 to 6
Outputs:
- basis_block: float32 [8, 16, 1728], P('ax', None, 'rad')
- coefficients: float32 [32, 16], replicated
- upper: float32 [16, 16], replicated
All inputs are finite; a program needn't handle non-finite values. No bound on the sum of `pattern` on one device may be relied on, other than what follows from the above.
Results may differ from a plain program's by a relative error of at most 0.0003.
Values sent between devices are 32-bit elements; how exact they have to be, the bound alone decides.
A program may use at most 128 MiB of HBM per device.

v0:
```python
import jax
import jax.numpy as jnp
from jax import lax
from jax.sharding import PartitionSpec as P

NRHS = 16


precise = lax.Precision.HIGHEST


def passed_along(value, axis, steps):
    count = lax.axis_size(axis)
    first, last = (max(0, -steps), min(count, count - steps))
    return lax.ppermute(value, axis, [(source, source + steps) for source in range(first, last)])


def apply_factor(factor, vectors):
    return jnp.einsum("rc,kc->kr", factor, vectors, precision=precise)


def body(couplings, pivots, pattern, krylov):
    rows_here = krylov.shape[2]
    width = couplings.shape[3]
    field_count = pattern.shape[3]
    points = width // field_count
    blocks = lax.axis_size("ax")
    levels = blocks.bit_length() - 1
    offset = lax.axis_index("rad") * rows_here
    row_field = (offset + jnp.arange(rows_here, dtype=jnp.int32)) // points
    col_field = jnp.arange(width, dtype=jnp.int32) // points
    field_ids = jnp.arange(field_count, dtype=jnp.int32)
    row_onehot = (row_field[:, None] == field_ids[None, :]).astype(jnp.float32)
    col_onehot = (field_ids[:, None] == col_field[None, :]).astype(jnp.float32)

    def masked(kind):
        field_mask = pattern[0, kind].astype(jnp.float32)
        keep = jnp.dot(
            jnp.dot(row_onehot, field_mask, precision=precise), col_onehot, precision=precise
        )
        return couplings[0, kind].astype(jnp.float32) * keep

    residue = krylov[0, krylov.shape[1] - NRHS :, :]
    for rung in range(levels):
        stride = 1 << rung
        whole_rows = lax.all_gather(residue, "rad", axis=1, tiled=True)
        push_high = apply_factor(masked(2 * rung), whole_rows)
        push_low = apply_factor(masked(2 * rung + 1), whole_rows)
        from_below = passed_along(push_high, "ax", stride)
        from_above = passed_along(push_low, "ax", -stride)
        residue = residue - from_below - from_above
    whole_final = lax.all_gather(residue, "rad", axis=1, tiled=True)
    solution = apply_factor(pivots[0], whole_final)
    rows_total = blocks * width
    stored = krylov[0]
    products = jnp.einsum("kb,rb->kr", stored, solution, precision=precise)
    solution_terms = jnp.einsum("rb,sb->rs", solution, solution, precision=precise)
    stored_terms = jnp.einsum("kb,jb->kj", stored, stored, precision=precise)
    summed, solution_gram, stored_gram = lax.psum(
        (products, solution_terms, stored_terms), ("ax", "rad")
    )
    coefficients = summed / rows_total
    remainder = solution - jnp.einsum("kr,kb->rb", coefficients, stored, precision=precise)
    cross = jnp.einsum("kr,ks->rs", coefficients, summed, precision=precise)
    inner = jnp.einsum("kr,kj,js->rs", coefficients, stored_gram, coefficients, precision=precise)
    gram = (solution_gram - cross - cross.T + inner) / rows_total
    lower = jnp.linalg.cholesky(gram)
    basis_rows = lax.linalg.triangular_solve(lower, remainder, left_side=True, lower=True)
    return (basis_rows[None], coefficients, lower.T)


def solution(mesh):
    return jax.shard_map(
        body,
        mesh=mesh,
        in_specs=(
            P("ax", None, "rad", None),
            P("ax", "rad", None),
            P("ax", None, None, None),
            P("ax", None, "rad"),
        ),
        out_specs=(P("ax", None, "rad"), P(), P()),
        check_vma=False,
    )
```

profile of v0, /device:TPU:0, one launch (start us, length us, event | category | flops | bytes accessed | tf_op | source)
XLA Modules:
  0.0 177.5 jit_solution(8327001351973904197)
XLA Ops:
  2.6 22.5 %all-gather = f32[1,16,1728]{1,0,2:T(1,128)S(1)} all-gather(f32[1,16,432]{1,0,2:T(1,128)S(1)} %copy.33), channel_id=2, replica_groups=mesh['ax'=8,'rad'=4] {'rad'}, dimensions={2}, use_global_device_ids=true | all-gather | bytes 138240 | tf_op jit(solution)/shard_map/all_gather | solution.py:46
  25.4 2.9 %convolution_multiply_fusion.5 = f32[432,1728]{1,0:T(8,128)S(1)} fusion(f32[432,9]{0,1:T(8,128)S(1)} %fusion.8, bf16[1,6,432,1728]{3,2,1,0:T(8,128)(2,1)} %param.4, s32[1728]{0:T(1024)S(1)} %add_select_fusion), kind=kOutput, calls=%fused_computation.5 | convolution fusion | flops 82130112 | bytes 4501440 | tf_op jit(solution)/shard_map/dot_general | solution.py:38
  28.4 2.8 %convolution_bitcast_fusion.2 = f32[16,432]{1,0:T(8,128)S(1)} fusion(f32[432,1728]{1,0:T(8,128)S(1)} %convolution_multiply_fusion.5, f32[16,1728]{0,1:T(8,128)S(1)} %bitcast.121), kind=kOutput, calls=%fused_computation.11 | convolution fusion | flops 143327232 | bytes 3124224 | tf_op jit(solution)/shard_map/rc,kc->kr/dot_general | solution.py:19
  32.8 1.5 convolution_multiply_fusion.4
  34.3 2.8 %convolution_bitcast_fusion.1 = f32[16,432]{1,0:T(8,128)S(1)} fusion(f32[432,1728]{1,0:T(8,128)S(1)} %convolution_multiply_fusion.4, f32[16,1728]{0,1:T(8,128)S(1)} %bitcast.122), kind=kOutput, calls=%fused_computation.10 | convolution fusion | flops 143327232 | bytes 3124224 | tf_op jit(solution)/shard_map/rc,kc->kr/dot_general | solution.py:19
  37.2 1.5 collective-permute-start.1
  39.0 3.2 %convolution_multiply_fusion.3 = f32[432,1728]{1,0:T(8,128)} fusion(f32[432,9]{0,1:T(8,128)S(1)} %fusion.6, bf16[1,6,432,1728]{3,2,1,0:T(8,128)(2,1)S(1)} %copy-done.3, s32[1728]{0:T(1024)S(1)} %add_select_fusion), kind=kOutput, calls=%fused_computation.3 | convolution fusion | flops 82130112 | bytes 4501440 | tf_op jit(solution)/shard_map/dot_general | solution.py:38
  42.5 3.2 %convolution_multiply_fusion.2 = f32[432,1728]{1,0:T(8,128)} fusion(f32[432,9]{0,1:T(8,128)S(1)} %fusion.5, bf16[1,6,432,1728]{3,2,1,0:T(8,128)(2,1)S(1)} %copy-done.3, s32[1728]{0:T(1024)S(1)} %add_select_fusion), kind=kOutput, calls=%fused_computation.2 | convolution fusion | flops 82130112 | bytes 4501440 | tf_op jit(solution)/shard_map/dot_general | solution.py:38
  46.0 3.1 %convolution_multiply_fusion.1 = f32[432,1728]{1,0:T(8,128)} fusion(f32[432,9]{0,1:T(8,128)S(1)} %fusion.4, bf16[1,6,432,1728]{3,2,1,0:T(8,128)(2,1)S(1)} %copy-done.3, s32[1728]{0:T(1024)S(1)} %add_select_fusion), kind=kOutput, calls=%fused_computation.1 | convolution fusion | flops 82130112 | bytes 4501440 | tf_op jit(solution)/shard_map/dot_general | solution.py:38
  49.6 13.7 %all-gather.1 = f32[4,432,16]{1,2,0:T(8,128)S(1)} all-gather(f32[1,432,16]{1,2,0:T(8,128)S(1)} %bitcast.123), channel_id=1, replica_groups=mesh['ax'=8,'rad'=4] {'rad'}, dimensions={0}, use_global_device_ids=true | all-gather | bytes 138240 | tf_op jit(solution)/shard_map/all_gather | solution.py:46
  63.5 4.6 %fusion.47 = f32[16,432]{1,0:T(8,128)S(1)} fusion(f32[1728,16]{0,1:T(8,128)S(1)} %reshape.66, f32[432,1728]{1,0:T(8,128)} %convolution_multiply_fusion.3), kind=kOutput, calls=%fused_computation.81 | convolution fusion | flops 143327232 | bytes 3124224 | tf_op jit(solution)/shard_map/rc,kc->kr/dot_general | solution.py:19
  68.1 6.1 %collective-permute-start.2 = (f32[16,432]{1,0:T(8,128)S(1)}, f32[16,432]{1,0:T(8,128)S(1)}, u32[]{:S(2)}, u32[]{:S(2)}) collective-permute-start(f32[16,432]{1,0:T(8,128)S(1)} %fusion.47), channel_id=1, source_target_pairs={{0,8},{4,12},{8,16},{12,20},{16,24},{20,28},{1,9},{5,13},{9,17},{1... | collective-permute-start | bytes 82952 | tf_op jit(solution)/shard_map/ppermute | solution.py:15
  74.2 2.6 %fusion.48 = f32[16,432]{1,0:T(8,128)S(1)} fusion(f32[1728,16]{0,1:T(8,128)S(1)} %reshape.66, f32[432,1728]{1,0:T(8,128)S(1)} %copy-done.1), kind=kOutput, calls=%fused_computation.82 | convolution fusion | flops 143327232 | bytes 3124224 | tf_op jit(solution)/shard_map/rc,kc->kr/dot_general | solution.py:19
  76.8 1.3 collective-permute-start.3
  78.2 4.5 %convolution_multiply_fusion = f32[432,1728]{1,0:T(8,128)} fusion(f32[432,9]{0,1:T(8,128)S(1)} %fusion.3, bf16[1,6,432,1728]{3,2,1,0:T(8,128)(2,1)} %param.4, s32[1728]{0:T(1024)S(1)} %add_select_fusion), kind=kOutput, calls=%fused_computation | convolution fusion | flops 82130112 | bytes 4501440 | tf_op jit(solution)/shard_map/dot_general | solution.py:38
  83.2 13.6 %all-gather.2 = f32[4,432,16]{1,2,0:T(8,128)S(1)} all-gather(f32[1,432,16]{1,2,0:T(8,128)S(1)} %fusion.45), channel_id=1, replica_groups=mesh['ax'=8,'rad'=4] {'rad'}, dimensions={0}, use_global_device_ids=true | all-gather | bytes 138240 | tf_op jit(solution)/shard_map/all_gather | solution.py:46
  97.0 4.6 %fusion.49 = f32[16,432]{1,0:T(8,128)S(1)} fusion(f32[1728,16]{0,1:T(8,128)S(1)} %reshape.68, f32[432,1728]{1,0:T(8,128)} %convolution_multiply_fusion.1), kind=kOutput, calls=%fused_computation.83 | convolution fusion | flops 143327232 | bytes 3124224 | tf_op jit(solution)/shard_map/rc,kc->kr/dot_general | solution.py:19
  101.6 6.1 %collective-permute-start.4 = (f32[16,432]{1,0:T(8,128)S(1)}, f32[16,432]{1,0:T(8,128)S(1)}, u32[]{:S(2)}, u32[]{:S(2)}) collective-permute-start(f32[16,432]{1,0:T(8,128)S(1)} %fusion.49), channel_id=1, source_target_pairs={{0,16},{4,20},{8,24},{12,28},{1,17},{5,21},{9,25},{13,29},{2,18},{... | collective-permute-start | bytes 82952 | tf_op jit(solution)/shard_map/ppermute | solution.py:15
  107.7 2.6 %fusion.50 = f32[16,432]{1,0:T(8,128)S(1)} fusion(f32[1728,16]{0,1:T(8,128)S(1)} %reshape.68, f32[432,1728]{1,0:T(8,128)S(1)} %copy-done.2), kind=kOutput, calls=%fused_computation.84 | convolution fusion | flops 143327232 | bytes 3124224 | tf_op jit(solution)/shard_map/rc,kc->kr/dot_general | solution.py:19
  111.9 4.3 %collective-permute-done.5 = f32[16,432]{1,0:T(8,128)S(1)} collective-permute-done((f32[16,432]{1,0:T(8,128)S(1)}, f32[16,432]{1,0:T(8,128)S(1)}, u32[]{:S(2)}, u32[]{:S(2)}) %collective-permute-start.5) | collective-permute-done | bytes 27680 | tf_op jit(solution)/shard_map/ppermute | solution.py:15
  116.2 13.3 %all-gather.3 = f32[4,432,16]{1,2,0:T(8,128)S(1)} all-gather(f32[1,432,16]{1,2,0:T(8,128)S(1)} %subtract_bitcast_fusion), channel_id=1, replica_groups=mesh['ax'=8,'rad'=4] {'rad'}, dimensions={0}, use_global_device_ids=true | all-gather | bytes 138240 | tf_op jit(solution)/shard_map/all_gather | solution.py:52
  129.8 2.6 %fusion = f32[16,432]{1,0:T(8,128)S(1)} fusion(f32[1728,16]{0,1:T(8,128)S(1)} %reshape.70, f32[1,432,1728]{2,1,0:T(8,128)S(1)} %copy-done), kind=kOutput, calls=%fused_computation.6 | convolution fusion | flops 143327232 | bytes 3124224 | tf_op jit(solution)/shard_map/rc,kc->kr/dot_general | solution.py:19
  132.8 38.4 %all-reduce = (f32[32,16]{0,1:T(8,128)S(1)}, f32[32,32]{1,0:T(8,128)S(1)}, f32[16,16]{0,1:T(8,128)S(1)}) all-reduce(f32[32,16]{0,1:T(8,128)S(1)} %convolution_bitcast_fusion.3, f32[32,32]{1,0:T(8,128)S(1)} %fusion.16, f32[16,16]{0,1:T(8,128)S(1)} %fusion.51), channel_id=1, replica_groups=mesh['ax'=8,'rad'=4] {'ax','rad'}, use_global_device_ids=true, to_apply=%region_1.2 | all-reduce | flops 1792 | bytes 14336 | tf_op jit(solution)/shard_map/psum | solution.py:59
  172.0 1.5 cholesky.16
  (56 shorter events, 13.0 us)
Async XLA Ops:
  0.6 129.2 %copy-start = (f32[1,432,1728]{2,1,0:T(8,128)S(1)}, f32[1,432,1728]{2,1,0:T(8,128)}, u32[]{:S(2)}) copy-start(f32[1,432,1728]{2,1,0:T(8,128)} %param.5) | copy-start | bytes 8957956
  2.6 30.2 %copy-start.3 = (bf16[1,6,432,1728]{3,2,1,0:T(8,128)(2,1)S(1)}, bf16[1,6,432,1728]{3,2,1,0:T(8,128)(2,1)}, u32[]{:S(2)}) copy-start(bf16[1,6,432,1728]{3,2,1,0:T(8,128)(2,1)} %param.4) | copy-start | bytes 26873860
  31.2 18.3 %collective-permute-start = (f32[16,432]{1,0:T(8,128)S(1)}, f32[16,432]{1,0:T(8,128)S(1)}, u32[]{:S(2)}, u32[]{:S(2)}) collective-permute-start(f32[16,432]{1,0:T(8,128)S(1)} %convolution_bitcast_fusion.2), channel_id=1, source_target_pairs={{0,4},{4,8},{8,12},{12,16},{16,20},{20,24},{24,28},{1,5},{5,9},{9,... | collective-permute-start | bytes 82952 | tf_op jit(solution)/shard_map/ppermute | solution.py:15
  37.2 12.4 %collective-permute-start.1 = (f32[16,432]{1,0:T(8,128)S(1)}, f32[16,432]{1,0:T(8,128)S(1)}, u32[]{:S(2)}, u32[]{:S(2)}) collective-permute-start(f32[16,432]{1,0:T(8,128)S(1)} %convolution_bitcast_fusion.1), channel_id=1, source_target_pairs={{4,0},{8,4},{12,8},{16,12},{20,16},{24,20},{28,24},{5,1},{9,5},{13... | collective-permute-start | bytes 82952 | tf_op jit(solution)/shard_map/ppermute | solution.py:15
  45.7 3.8 %copy-start.4 = (f32[1,32,432]{2,1,0:T(8,128)S(1)}, f32[1,32,432]{2,1,0:T(8,128)}, u32[]{:S(2)}) copy-start(f32[1,32,432]{2,1,0:T(8,128)} %param.7) | copy-start | bytes 165892
  63.5 10.7 %copy-start.1 = (f32[432,1728]{1,0:T(8,128)S(1)}, f32[432,1728]{1,0:T(8,128)}, u32[]{:S(2)}) copy-start(f32[432,1728]{1,0:T(8,128)} %convolution_multiply_fusion.2) | copy-start | bytes 8957956
  68.1 14.6 %collective-permute-start.2 = (f32[16,432]{1,0:T(8,128)S(1)}, f32[16,432]{1,0:T(8,128)S(1)}, u32[]{:S(2)}, u32[]{:S(2)}) collective-permute-start(f32[16,432]{1,0:T(8,128)S(1)} %fusion.47), channel_id=1, source_target_pairs={{0,8},{4,12},{8,16},{12,20},{16,24},{20,28},{1,9},{5,13},{9,17},{1... | collective-permute-start | bytes 82952 | tf_op jit(solution)/shard_map/ppermute | solution.py:15
  76.8 6.3 %collective-permute-start.3 = (f32[16,432]{1,0:T(8,128)S(1)}, f32[16,432]{1,0:T(8,128)S(1)}, u32[]{:S(2)}, u32[]{:S(2)}) collective-permute-start(f32[16,432]{1,0:T(8,128)S(1)} %fusion.48), channel_id=1, source_target_pairs={{8,0},{12,4},{16,8},{20,12},{24,16},{28,20},{9,1},{13,5},{17,9},{2... | collective-permute-start | bytes 82952 | tf_op jit(solution)/shard_map/ppermute | solution.py:15
  97.0 10.7 %copy-start.2 = (f32[432,1728]{1,0:T(8,128)S(1)}, f32[432,1728]{1,0:T(8,128)}, u32[]{:S(2)}) copy-start(f32[432,1728]{1,0:T(8,128)} %convolution_multiply_fusion) | copy-start | bytes 8957956
  101.6 10.3 %collective-permute-start.4 = (f32[16,432]{1,0:T(8,128)S(1)}, f32[16,432]{1,0:T(8,128)S(1)}, u32[]{:S(2)}, u32[]{:S(2)}) collective-permute-start(f32[16,432]{1,0:T(8,128)S(1)} %fusion.49), channel_id=1, source_target_pairs={{0,16},{4,20},{8,24},{12,28},{1,17},{5,21},{9,25},{13,29},{2,18},{... | collective-permute-start | bytes 82952 | tf_op jit(solution)/shard_map/ppermute | solution.py:15
  110.3 5.8 %collective-permute-start.5 = (f32[16,432]{1,0:T(8,128)S(1)}, f32[16,432]{1,0:T(8,128)S(1)}, u32[]{:S(2)}, u32[]{:S(2)}) collective-permute-start(f32[16,432]{1,0:T(8,128)S(1)} %fusion.50), channel_id=1, source_target_pairs={{16,0},{20,4},{24,8},{28,12},{17,1},{21,5},{25,9},{29,13},{18,2},{... | collective-permute-start | bytes 82952 | tf_op jit(solution)/shard_map/ppermute | solution.py:15
  171.2 6.3 %copy-start.5 = (f32[32,16]{0,1:T(8,128)}, f32[32,16]{0,1:T(8,128)S(1)}, u32[]{:S(2)}) copy-start(f32[32,16]{0,1:T(8,128)S(1)} %broadcast_multiply_fusion) | copy-start | bytes 6148
where the time goes:
time: 178 us
  blocking collectives  102 us (57%)
  matrix products  45.2 us (25%)
  starting transfers between devices  17.5 us (10%)
  waiting for transfers between devices  4.77 us (3%)
  other arithmetic  4.08 us (2%)
  local copies, waits for them, and re-layouts  3.46 us (2%)
    all_gather x3, blocking collectives, body(): whole_rows = lax.all_gather(residue, 'rad', axis=1, tiled=True)  49.7 us
    psum x1, blocking collectives, body(): lax.psum((products, solution_terms, stored_terms), ('ax', 'rad'))  38.4 us
    dot_general x7, matrix products, apply_factor(): return jnp.einsum('rc,kc->kr', factor, vectors, precision=precise)  22.8 us
    dot_general x6, matrix products, masked(): jnp.dot(jnp.dot(row_onehot, field_mask, precision=precise), col_onehot, p...  18.5 us
    ppermute x6, starting transfers between devices, passed_along(): lax.ppermute(value, axis, [(source, source + steps) for source in range(f...  17.5 us
    all_gather x1, blocking collectives, body(): whole_final = lax.all_gather(residue, 'rad', axis=1, tiled=True)  13.3 us
    ppermute x6, waiting for transfers between devices, passed_along(): lax.ppermute(value, axis, [(source, source + steps) for source in range(f...  4.77 us
  transfers between devices with their start and end apart: 6, of which 2 were waited for; matrix products, arithmetic and copies ran while one was open for 14% of the time, Pallas kernels for 0%

commit v1 on v0

v1 whole, which is shorter than its diff:
```python
import functools
import math

import jax
import jax.numpy as jnp
from jax import lax
from jax.experimental import pallas as pl
from jax.experimental.pallas import tpu as pltpu
from jax.sharding import PartitionSpec as P

NRHS = 16
SUBLANES = 8
LANES = 128
MESH = pl.DeviceIdType.MESH

precise = lax.Precision.HIGHEST


def dot_nt(a, b, precision=None):
    return lax.dot_general(
        a, b, (((1,), (1,)), ((), ())), precision=precision, preferred_element_type=jnp.float32
    )


def pack(matrix):
    groups = matrix.shape[0] // SUBLANES
    slot = LANES // groups
    parts = []
    for group in range(groups):
        parts.append(matrix[group * SUBLANES : (group + 1) * SUBLANES])
        if slot > matrix.shape[1]:
            parts.append(jnp.zeros((SUBLANES, slot - matrix.shape[1]), jnp.float32))
    return jnp.concatenate(parts, axis=1)


def unpack(tile, shape):
    groups = shape[0] // SUBLANES
    slot = LANES // groups
    return jnp.concatenate(
        [tile[:, group * slot : group * slot + shape[1]] for group in range(groups)], axis=0
    )


def halves(value):
    high = value.astype(jnp.bfloat16)
    low = (value - high.astype(jnp.float32)).astype(jnp.bfloat16)
    return high, low


def kernel(
    blocks, ranks, couplings, pivots, pattern, krylov, basis, coefficients, upper,
    factors, pivot_in, pivot_high, pivot_low, keep, pieces, inbox,
    tile_rad, tile_ax, load_sem, piece_send, piece_recv, push_send, push_recv,
    rad_send, rad_recv, ax_send, ax_recv,
):
    kinds, rows_here, width = factors.shape
    levels = kinds // 2
    stored_count = krylov.shape[1]
    fields = pattern.shape[3]
    points = width // fields
    rows_total = blocks * width
    me = lax.axis_index("ax")
    rank = lax.axis_index("rad")

    def load(kind):
        return pltpu.make_async_copy(couplings.at[0, kind], factors.at[kind], load_sem.at[kind])

    load_pivots = pltpu.make_async_copy(pivots.at[0], pivot_in, load_sem.at[kinds])
    for kind in range(kinds):
        load(kind).start()
    load_pivots.start()

    barrier = pltpu.get_barrier_semaphore()
    for step in range(1, ranks):
        pl.semaphore_signal(
            barrier, inc=1, device_id=(me, lax.rem(rank + step, ranks)), device_id_type=MESH
        )
    for step in range(1, blocks):
        pl.semaphore_signal(
            barrier, inc=1, device_id=(lax.rem(me + step, blocks), rank), device_id_type=MESH
        )
    pieces[0, rank] = krylov[0, stored_count - NRHS :, :]

    col_field = lax.broadcasted_iota(jnp.int32, (fields, width), 1) // points
    col_onehot = (col_field == lax.broadcasted_iota(jnp.int32, (fields, width), 0)).astype(
        jnp.float32
    )
    for kind in range(kinds):
        keep[kind] = jnp.dot(
            pattern[0, kind].astype(jnp.float32), col_onehot, preferred_element_type=jnp.float32
        )
    pl.semaphore_wait(barrier, ranks + blocks - 2)

    def piece_copy(level, step):
        return pltpu.make_async_remote_copy(
            src_ref=pieces.at[level, rank],
            dst_ref=pieces.at[level, rank],
            send_sem=piece_send.at[level, step],
            recv_sem=piece_recv.at[level, rank],
            device_id=(me, lax.rem(rank + step, ranks)),
            device_id_type=MESH,
        )

    def piece_arrival(level, step):
        source = lax.rem(rank + step, ranks)
        return pltpu.make_async_remote_copy(
            src_ref=pieces.at[level, source],
            dst_ref=pieces.at[level, source],
            send_sem=piece_send.at[level, step],
            recv_sem=piece_recv.at[level, source],
            device_id=(me, source),
            device_id_type=MESH,
        )

    def push_copy(level, way):
        stride = 1 << level
        target = me + stride if way == 0 else me - stride
        return pltpu.make_async_remote_copy(
            src_ref=inbox.at[level, 2 + way],
            dst_ref=inbox.at[level, way],
            send_sem=push_send.at[level, way],
            recv_sem=push_recv.at[level, way],
            device_id=(target, rank),
            device_id_type=MESH,
        )

    def rad_copy(which, step):
        return pltpu.make_async_remote_copy(
            src_ref=tile_rad.at[which, rank],
            dst_ref=tile_rad.at[which, rank],
            send_sem=rad_send.at[which, step],
            recv_sem=rad_recv.at[which, rank],
            device_id=(me, lax.rem(rank + step, ranks)),
            device_id_type=MESH,
        )

    def rad_arrival(which, step):
        source = lax.rem(rank + step, ranks)
        return pltpu.make_async_remote_copy(
            src_ref=tile_rad.at[which, source],
            dst_ref=tile_rad.at[which, source],
            send_sem=rad_send.at[which, step],
            recv_sem=rad_recv.at[which, source],
            device_id=(me, source),
            device_id_type=MESH,
        )

    def ax_copy(which, step):
        return pltpu.make_async_remote_copy(
            src_ref=tile_ax.at[which, me],
            dst_ref=tile_ax.at[which, me],
            send_sem=ax_send.at[which, step],
            recv_sem=ax_recv.at[which, me],
            device_id=(lax.rem(me + step, blocks), rank),
            device_id_type=MESH,
        )

    def ax_arrival(which, step):
        source = lax.rem(me + step, blocks)
        return pltpu.make_async_remote_copy(
            src_ref=tile_ax.at[which, source],
            dst_ref=tile_ax.at[which, source],
            send_sem=ax_send.at[which, step],
            recv_sem=ax_recv.at[which, source],
            device_id=(source, rank),
            device_id_type=MESH,
        )

    def send_pieces(level):
        for step in range(1, ranks):
            piece_copy(level, step).start()

    def whole(level):
        for step in range(1, ranks):
            piece_arrival(level, step).wait_recv()
        return jnp.concatenate([pieces[level, source] for source in range(ranks)], axis=1)

    def reduce_start(which, matrix):
        tile_rad[which, rank] = pack(matrix)
        for step in range(1, ranks):
            rad_copy(which, step).start()

    def reduce_middle(which):
        for step in range(1, ranks):
            rad_arrival(which, step).wait_recv()
        total = tile_rad[which, 0]
        for source in range(1, ranks):
            total += tile_rad[which, source]
        tile_ax[which, me] = total
        for step in range(1, blocks):
            ax_copy(which, step).start()

    def reduce_end(which, shape):
        for step in range(1, blocks):
            ax_arrival(which, step).wait_recv()
        total = tile_ax[which, 0]
        for source in range(1, blocks):
            total += tile_ax[which, source]
        return unpack(total, shape)

    group = math.gcd(points, rows_here)

    def mask(kind):
        load(kind).wait()

        @pl.loop(0, rows_here // group)
        def _(index):
            field = (rank * rows_here + index * group) // points
            row = keep[kind, pl.ds(field, 1), :]
            rows = pl.ds(pl.multiple_of(index * group, group), group)
            wide = jnp.broadcast_to(row, (group, width)).astype(jnp.bfloat16)
            factors[kind, rows, :] = factors[kind, rows, :] * wide

    def split_pivots():
        load_pivots.wait()

        @pl.loop(0, rows_here // group)
        def _(index):
            rows = pl.ds(pl.multiple_of(index * group, group), group)
            high, low = halves(pivot_in[rows, :])
            pivot_high[rows, :] = high
            pivot_low[rows, :] = low

    send_pieces(0)
    stored = krylov[0]
    reduce_start(0, dot_nt(stored, stored, precise))
    mask(0)
    mask(1)

    for level in range(levels):
        stride = 1 << level
        has_higher = me + stride < blocks
        has_lower = me >= stride
        both = jnp.concatenate(halves(whole(level)), axis=0)
        for way, has_target in ((0, has_higher), (1, has_lower)):
            product = dot_nt(both, factors[2 * level + way])
            inbox[level, 2 + way] = product[:NRHS] + product[NRHS:]

            @pl.when(has_target)
            def _():
                push_copy(level, way).start()

        if level + 1 < levels:
            mask(2 * level + 2)
        else:
            split_pivots()
        pieces[level + 1, rank] = pieces[level, rank]
        for way, has_source in ((0, has_lower), (1, has_higher)):

            @pl.when(has_source)
            def _():
                push_copy(level, way).wait_recv()
                pieces[level + 1, rank] = pieces[level + 1, rank] - inbox[level, way]

        send_pieces(level + 1)
        if level == 0:
            reduce_middle(0)
        if level + 1 < levels:
            mask(2 * level + 3)

    stored_gram = reduce_end(0, (stored_count, stored_count)) / rows_total
    diagonal = lax.broadcasted_iota(jnp.int32, (stored_count, stored_count), 0) == (
        lax.broadcasted_iota(jnp.int32, (stored_count, stored_count), 1)
    )
    middle = stored_gram - jnp.where(diagonal, 2.0, 0.0)

    high, low = halves(whole(levels))
    product = dot_nt(jnp.concatenate([high, low], axis=0), pivot_high[...])
    x = product[:NRHS] + product[NRHS:] + dot_nt(high, pivot_low[...])
    reduce_start(1, dot_nt(x, jnp.concatenate([stored, x], axis=0), precise))
    reduce_middle(1)
    sums = reduce_end(1, (NRHS, stored_count + NRHS)) / rows_total
    shares = sums[:, :stored_count]
    coefficients[...] = shares.T
    gram = sums[:, stored_count:] + dot_nt(
        jnp.dot(shares, middle, precision=precise, preferred_element_type=jnp.float32),
        shares,
        precise,
    )
    remainder = x - jnp.dot(shares, stored, precision=precise, preferred_element_type=jnp.float32)

    row_id = lax.broadcasted_iota(jnp.int32, (NRHS, 2 * NRHS), 0)
    col_id = lax.broadcasted_iota(jnp.int32, (NRHS, 2 * NRHS), 1)
    table = jnp.concatenate(
        [gram, (row_id == col_id)[:, :NRHS].astype(jnp.float32)], axis=1
    )
    for step in range(NRHS - 1):
        pivot_row = table[step : step + 1, :]
        factor = table[:, step : step + 1] / table[step : step + 1, step : step + 1]
        table = table - jnp.where(row_id > step, factor * pivot_row, 0.0)
    scale = jnp.sqrt(jnp.sum(jnp.where(row_id == col_id, table, 0.0), axis=1, keepdims=True))
    table = table / scale
    upper[...] = jnp.where(row_id <= col_id, table, 0.0)[:, :NRHS]
    basis[0] = jnp.dot(
        table[:, NRHS:], remainder, precision=precise, preferred_element_type=jnp.float32
    )

    for level in range(levels + 1):
        for step in range(1, ranks):
            piece_copy(level, step).wait_send()
    for level in range(levels):
        stride = 1 << level
        for way, has_target in ((0, me + stride < blocks), (1, me >= stride)):

            @pl.when(has_target)
            def _():
                push_copy(level, way).wait_send()

    for which in range(2):
        for step in range(1, ranks):
            rad_copy(which, step).wait_send()
        for step in range(1, blocks):
            ax_copy(which, step).wait_send()


def body(couplings, pivots, pattern, krylov):
    kinds, rows_here, width = couplings.shape[1:]
    blocks = lax.axis_size("ax")
    ranks = lax.axis_size("rad")
    fields = pattern.shape[3]
    levels = kinds // 2
    stored_count = krylov.shape[1]
    vmem = pl.BlockSpec(memory_space=pltpu.VMEM)
    hbm = pl.BlockSpec(memory_space=pl.ANY)
    dma = pltpu.SemaphoreType.DMA
    return pl.pallas_call(
        functools.partial(kernel, blocks, ranks),
        out_shape=(
            jax.ShapeDtypeStruct((1, NRHS, rows_here), jnp.float32),
            jax.ShapeDtypeStruct((stored_count, NRHS), jnp.float32),
            jax.ShapeDtypeStruct((NRHS, NRHS), jnp.float32),
        ),
        in_specs=[hbm, hbm, vmem, vmem],
        out_specs=(vmem, vmem, vmem),
        scratch_shapes=[
            pltpu.VMEM((kinds, rows_here, width), jnp.bfloat16),
            pltpu.VMEM((rows_here, width), jnp.float32),
            pltpu.VMEM((rows_here, width), jnp.bfloat16),
            pltpu.VMEM((rows_here, width), jnp.bfloat16),
            pltpu.VMEM((kinds, fields, width), jnp.float32),
            pltpu.VMEM((levels + 1, ranks, NRHS, rows_here), jnp.float32),
            pltpu.VMEM((levels, 4, NRHS, rows_here), jnp.float32),
            pltpu.VMEM((2, ranks, SUBLANES, LANES), jnp.float32),
            pltpu.VMEM((2, blocks, SUBLANES, LANES), jnp.float32),
            dma((kinds + 1,)),
            dma((levels + 1, ranks)),
            dma((levels + 1, ranks)),
            dma((levels, 2)),
            dma((levels, 2)),
            dma((2, ranks)),
            dma((2, ranks)),
            dma((2, blocks)),
            dma((2, blocks)),
        ],
        compiler_params=pltpu.CompilerParams(
            collective_id=0, has_side_effects=True, vmem_limit_bytes=48 * 1024 * 1024
        ),
    )(couplings, pivots, pattern, krylov)


def solution(mesh):
    return jax.shard_map(
        body,
        mesh=mesh,
        in_specs=(
            P("ax", None, "rad", None),
            P("ax", "rad", None),
            P("ax", None, None, None),
            P("ax", None, "rad"),
        ),
        out_specs=(P("ax", None, "rad"), P(), P()),
        check_vma=False,
    )
```

time: 178 us -> 51 us (0.29)
  blocking collectives: 102 us -> 0 us
  matrix products: 45.2 us -> 0 us
  Pallas kernels: 0 us -> 44.8 us
  starting transfers between devices: 17.5 us -> 0 us
  waiting for transfers between devices: 4.77 us -> 0 us
  other arithmetic: 4.08 us -> 0 us
  local copies, waits for them, and re-layouts: 3.46 us -> 5.35 us
    all_gather x4 -> x0, blocking collectives: 63.1 us -> none  [the longest x3 49.7 us: body(): whole_rows = lax.all_gather(residue, 'rad', axis=1, tiled=True)]
    pallas_call x0 -> x1, Pallas kernels: none -> 44.8 us  [body(): pl.pallas_call(functools.partial(kernel, blocks, ranks), out_shape=(jax.S...]
    dot_general x26 -> x0, matrix products: 44.3 us -> none  [the longest x7 22.8 us: apply_factor(): return jnp.einsum('rc,kc->kr', factor, vectors, precision=precise)]
    psum x1 -> x0, blocking collectives: 38.4 us -> none  [body(): lax.psum((products, solution_terms, stored_terms), ('ax', 'rad'))]
    ppermute x6 -> x0, starting transfers between devices: 17.5 us -> none  [passed_along(): lax.ppermute(value, axis, [(source, source + steps) for source in range(f...]
    ppermute x6 -> x0, waiting for transfers between devices: 4.77 us -> none  [passed_along(): lax.ppermute(value, axis, [(source, source + steps) for source in range(f...]
    unnamed x16 -> x7, local copies, waits for them, and re-layouts: 1.18 us -> 4.68 us
    another operation x4 -> x0, other arithmetic: 3.37 us -> none  [the longest x3 2.14 us: body(): lower = jnp.linalg.cholesky(gram)]
  transfers between devices with their start and end apart: 6 -> 0, of which waited for: 2 -> 0; matrix products, arithmetic and copies ran while one was open for 14% -> 0% of each run, Pallas kernels for 0% -> 0%
where the time goes in v1:
time: 51 us; the launch traced here: 50.8 us
  Pallas kernels  44.8 us (88%)
  local copies, waits for them, and re-layouts  5.35 us (10%)
  between operations  0.64 us (1%)
    pallas_call x1, Pallas kernels, body(): pl.pallas_call(functools.partial(kernel, blocks, ranks), out_shape=(jax.S...  44.8 us
    unnamed x7, local copies, waits for them, and re-layouts  4.68 us

profile of v1, /device:TPU:0, one launch (start us, length us, event | category | flops | bytes accessed | tf_op | source)
XLA Modules:
  0.0 50.8 jit_solution(8515003876169428282)
XLA Ops:
  0.6 0.8 %copy.7.pattern = s32[1,6,9,9]{3,2,1,0:T(8,128)S(1)} copy(s32[1,6,9,9]{3,0,2,1:T(1,128)} %param.6) | data formatting | bytes 3888 | tf_op args[2]
  1.4 0.0 copy-start
  1.4 1.9 %copy-done = f32[1,432,1728]{2,1,0:T(8,128)S(1)} copy-done((f32[1,432,1728]{2,1,0:T(8,128)S(1)}, f32[1,432,1728]{2,1,0:T(8,128)}, u32[]{:S(2)}) %copy-start) | copy-done | bytes 2986008
  3.3 0.0 copy-start.1
  3.3 0.8 %copy-done.1 = f32[1,32,432]{2,1,0:T(8,128)S(1)} copy-done((f32[1,32,432]{2,1,0:T(8,128)S(1)}, f32[1,32,432]{2,1,0:T(8,128)}, u32[]{:S(2)}) %copy-start.1) | copy-done | bytes 55320
  4.1 44.8 %shard_map.67 = (f32[1,16,432]{2,1,0:T(8,128)S(1)}, f32[32,16]{1,0:T(8,128)S(1)}, f32[16,16]{1,0:T(8,128)S(1)}) custom-call(bf16[1,6,432,1728]{3,2,1,0:T(8,128)(2,1)} %couplings.1, f32[1,432,1728]{2,1,0:T(8,128)S(1)} %copy-done, s32[1,6,9,9]{3,2,1,0:T(8,128)S(1)} %copy.7.pattern, f32[1,32,432]{2,1,0:T(8,128)S(1)} %copy-done.1), custom_call_target="tpu_custom_call" | custom-call | tf_op jit(solution)/shard_map/pallas_call | solution.py:326
  48.9 0.7 %copy.8 = f32[32,16]{0,1:T(8,128)} copy(f32[32,16]{1,0:T(8,128)S(1)} %get-tuple-element.4) | data formatting | bytes 4096 | tf_op jit(solution)/shard_map/pallas_call | solution.py:326
  49.6 0.6 %copy.11 = f32[1,16,432]{2,1,0:T(8,128)} copy(f32[1,16,432]{2,1,0:T(8,128)S(1)} %get-tuple-element.9) | data formatting | bytes 55296
  50.2 0.6 %copy.12 = f32[16,16]{1,0:T(8,128)} copy(f32[16,16]{1,0:T(8,128)S(1)} %get-tuple-element.11) | data formatting | bytes 2048
Async XLA Ops:
  1.4 1.9 %copy-start = (f32[1,432,1728]{2,1,0:T(8,128)S(1)}, f32[1,432,1728]{2,1,0:T(8,128)}, u32[]{:S(2)}) copy-start(f32[1,432,1728]{2,1,0:T(8,128)} %pivots.1) | copy-start | bytes 8957956
  3.3 0.8 %copy-start.1 = (f32[1,32,432]{2,1,0:T(8,128)S(1)}, f32[1,32,432]{2,1,0:T(8,128)}, u32[]{:S(2)}) copy-start(f32[1,32,432]{2,1,0:T(8,128)} %krylov.1) | copy-start | bytes 165892

commit v2 on v1

--- a/solution.py
+++ b/solution.py
@@ -11,6 +11,7 @@
 NRHS = 16
 SUBLANES = 8
 LANES = 128
+PART = 8
 MESH = pl.DeviceIdType.MESH
 
 precise = lax.Precision.HIGHEST
@@ -48,13 +49,14 @@
 
 
 def kernel(
-    blocks, ranks, couplings, pivots, pattern, krylov, basis, coefficients, upper,
-    factors, pivot_in, pivot_high, pivot_low, keep, pieces, inbox,
+    blocks, ranks, couplings, pivots, pattern_hbm, krylov_hbm, remainder_out, shares_out, table_out,
+    pattern, krylov, factors, pivot_in, pivot_high, pivot_low, keep, pieces, inbox,
     tile_rad, tile_ax, load_sem, piece_send, piece_recv, push_send, push_recv,
     rad_send, rad_recv, ax_send, ax_recv,
 ):
     kinds, rows_here, width = factors.shape
     levels = kinds // 2
+    parts = NRHS // PART
     stored_count = krylov.shape[1]
     fields = pattern.shape[3]
     points = width // fields
@@ -65,10 +67,13 @@
     def load(kind):
         return pltpu.make_async_copy(couplings.at[0, kind], factors.at[kind], load_sem.at[kind])
 
+    load_krylov = pltpu.make_async_copy(krylov_hbm, krylov, load_sem.at[kinds + 1])
+    load_pattern = pltpu.make_async_copy(pattern_hbm, pattern, load_sem.at[kinds + 2])
+    load_krylov.start()
+    load_pattern.start()
     load_pivots = pltpu.make_async_copy(pivots.at[0], pivot_in, load_sem.at[kinds])
-    for kind in range(kinds):
+    for kind in range(2):
         load(kind).start()
-    load_pivots.start()
 
     barrier = pltpu.get_barrier_semaphore()
     for step in range(1, ranks):
@@ -79,7 +84,11 @@
         pl.semaphore_signal(
             barrier, inc=1, device_id=(lax.rem(me + step, blocks), rank), device_id_type=MESH
         )
-    pieces[0, rank] = krylov[0, stored_count - NRHS :, :]
+    load_krylov.wait()
+    for part in range(parts):
+        first = stored_count - NRHS + part * PART
+        pieces[part, 0, rank] = krylov[0, first : first + PART, :]
+    load_pattern.wait()
 
     col_field = lax.broadcasted_iota(jnp.int32, (fields, width), 1) // points
     col_onehot = (col_field == lax.broadcasted_iota(jnp.int32, (fields, width), 0)).astype(
@@ -91,35 +100,35 @@
         )
     pl.semaphore_wait(barrier, ranks + blocks - 2)
 
-    def piece_copy(level, step):
-        return pltpu.make_async_remote_copy(
-            src_ref=pieces.at[level, rank],
-            dst_ref=pieces.at[level, rank],
-            send_sem=piece_send.at[level, step],
-            recv_sem=piece_recv.at[level, rank],
+    def piece_copy(part, level, step):
+        return pltpu.make_async_remote_copy(
+            src_ref=pieces.at[part, level, rank],
+            dst_ref=pieces.at[part, level, rank],
+            send_sem=piece_send.at[part, level, step],
+            recv_sem=piece_recv.at[part, level, rank],
             device_id=(me, lax.rem(rank + step, ranks)),
             device_id_type=MESH,
         )
 
-    def piece_arrival(level, step):
+    def piece_arrival(part, level, step):
         source = lax.rem(rank + step, ranks)
         return pltpu.make_async_remote_copy(
-            src_ref=pieces.at[level, source],
-            dst_ref=pieces.at[level, source],
-            send_sem=piece_send.at[level, step],
-            recv_sem=piece_recv.at[level, source],
+            src_ref=pieces.at[part, level, source],
+            dst_ref=pieces.at[part, level, source],
+            send_sem=piece_send.at[part, level, step],
+            recv_sem=piece_recv.at[part, level, source],
             device_id=(me, source),
             device_id_type=MESH,
         )
 
-    def push_copy(level, way):
+    def push_copy(part, level, way):
         stride = 1 << level
         target = me + stride if way == 0 else me - stride
         return pltpu.make_async_remote_copy(
-            src_ref=inbox.at[level, 2 + way],
-            dst_ref=inbox.at[level, way],
-            send_sem=push_send.at[level, way],
-            recv_sem=push_recv.at[level, way],
+            src_ref=inbox.at[part, level, 2 + way],
+            dst_ref=inbox.at[part, level, way],
+            send_sem=push_send.at[part, level, way],
+            recv_sem=push_recv.at[part, level, way],
             device_id=(target, rank),
             device_id_type=MESH,
         )
@@ -166,14 +175,14 @@
             device_id_type=MESH,
         )
 
-    def send_pieces(level):
+    def send_pieces(part, level):
         for step in range(1, ranks):
-            piece_copy(level, step).start()
-
-    def whole(level):
+            piece_copy(part, level, step).start()
+
+    def whole(part, level):
         for step in range(1, ranks):
-            piece_arrival(level, step).wait_recv()
-        return jnp.concatenate([pieces[level, source] for source in range(ranks)], axis=1)
+            piece_arrival(part, level, step).wait_recv()
+        return jnp.concatenate([pieces[part, level, source] for source in range(ranks)], axis=1)
 
     def reduce_start(which, matrix):
         tile_rad[which, rank] = pack(matrix)
@@ -201,7 +210,8 @@
     group = math.gcd(points, rows_here)
 
     def mask(kind):
-        load(kind).wait()
+        if kind != 1:
+            load(kind).wait()
 
         @pl.loop(0, rows_here // group)
         def _(index):
@@ -221,9 +231,14 @@
             pivot_high[rows, :] = high
             pivot_low[rows, :] = low
 
-    send_pieces(0)
+    for part in range(parts):
+        send_pieces(part, 0)
     stored = krylov[0]
     reduce_start(0, dot_nt(stored, stored, precise))
+    load(1).wait()
+    for kind in range(2, kinds):
+        load(kind).start()
+    load_pivots.start()
     mask(0)
     mask(1)
 
@@ -231,28 +246,32 @@
         stride = 1 << level
         has_higher = me + stride < blocks
         has_lower = me >= stride
-        both = jnp.concatenate(halves(whole(level)), axis=0)
-        for way, has_target in ((0, has_higher), (1, has_lower)):
-            product = dot_nt(both, factors[2 * level + way])
-            inbox[level, 2 + way] = product[:NRHS] + product[NRHS:]
-
-            @pl.when(has_target)
-            def _():
-                push_copy(level, way).start()
+        for part in range(parts):
+            both = jnp.concatenate(halves(whole(part, level)), axis=0)
+            for way, has_target in ((0, has_higher), (1, has_lower)):
+                product = dot_nt(both, factors[2 * level + way])
+                inbox[part, level, 2 + way] = product[:PART] + product[PART:]
+
+                @pl.when(has_target)
+                def _():
+                    push_copy(part, level, way).start()
 
         if level + 1 < levels:
             mask(2 * level + 2)
         else:
             split_pivots()
-        pieces[level + 1, rank] = pieces[level, rank]
-        for way, has_source in ((0, has_lower), (1, has_higher)):
-
-            @pl.when(has_source)
-            def _():
-                push_copy(level, way).wait_recv()
-                pieces[level + 1, rank] = pieces[level + 1, rank] - inbox[level, way]
-
-        send_pieces(level + 1)
+        for part in range(parts):
+            pieces[part, level + 1, rank] = pieces[part, level, rank]
+            for way, has_source in ((0, has_lower), (1, has_higher)):
+
+                @pl.when(has_source)
+                def _():
+                    push_copy(part, level, way).wait_recv()
+                    pieces[part, level + 1, rank] = (
+                        pieces[part, level + 1, rank] - inbox[part, level, way]
+                    )
+
+            send_pieces(part, level + 1)
         if level == 0:
             reduce_middle(0)
         if level + 1 < levels:
@@ -264,20 +283,23 @@
     )
     middle = stored_gram - jnp.where(diagonal, 2.0, 0.0)
 
-    high, low = halves(whole(levels))
-    product = dot_nt(jnp.concatenate([high, low], axis=0), pivot_high[...])
-    x = product[:NRHS] + product[NRHS:] + dot_nt(high, pivot_low[...])
+    solved = []
+    for part in range(parts):
+        high, low = halves(whole(part, levels))
+        product = dot_nt(jnp.concatenate([high, low], axis=0), pivot_high[...])
+        solved.append(product[:PART] + product[PART:] + dot_nt(high, pivot_low[...]))
+    x = jnp.concatenate(solved, axis=0)
     reduce_start(1, dot_nt(x, jnp.concatenate([stored, x], axis=0), precise))
     reduce_middle(1)
     sums = reduce_end(1, (NRHS, stored_count + NRHS)) / rows_total
     shares = sums[:, :stored_count]
-    coefficients[...] = shares.T
+    shares_out[...] = shares
     gram = sums[:, stored_count:] + dot_nt(
         jnp.dot(shares, middle, precision=precise, preferred_element_type=jnp.float32),
         shares,
         precise,
     )
-    remainder = x - jnp.dot(shares, stored, precision=precise, preferred_element_type=jnp.float32)
+    remainder_out[...] = x - jnp.dot(shares, stored, precision=precise, preferred_element_type=jnp.float32)
 
     row_id = lax.broadcasted_iota(jnp.int32, (NRHS, 2 * NRHS), 0)
     col_id = lax.broadcasted_iota(jnp.int32, (NRHS, 2 * NRHS), 1)
@@ -290,27 +312,37 @@
         table = table - jnp.where(row_id > step, factor * pivot_row, 0.0)
     scale = jnp.sqrt(jnp.sum(jnp.where(row_id == col_id, table, 0.0), axis=1, keepdims=True))
     table = table / scale
-    upper[...] = jnp.where(row_id <= col_id, table, 0.0)[:, :NRHS]
-    basis[0] = jnp.dot(
-        table[:, NRHS:], remainder, precision=precise, preferred_element_type=jnp.float32
-    )
-
-    for level in range(levels + 1):
-        for step in range(1, ranks):
-            piece_copy(level, step).wait_send()
+    table_out[...] = table
+
+    for part in range(parts):
+        for level in range(levels + 1):
+            for step in range(1, ranks):
+                piece_copy(part, level, step).wait_send()
     for level in range(levels):
         stride = 1 << level
         for way, has_target in ((0, me + stride < blocks), (1, me >= stride)):
 
             @pl.when(has_target)
             def _():
-                push_copy(level, way).wait_send()
+                for part in range(parts):
+                    push_copy(part, level, way).wait_send()
 
     for which in range(2):
         for step in range(1, ranks):
             rad_copy(which, step).wait_send()
         for step in range(1, blocks):
             ax_copy(which, step).wait_send()
+
+
+def finish(remainder, shares, table, basis, shares_out, upper):
+    values = table[...]
+    row_id = lax.broadcasted_iota(jnp.int32, (NRHS, NRHS), 0)
+    col_id = lax.broadcasted_iota(jnp.int32, (NRHS, NRHS), 1)
+    upper[...] = jnp.where(row_id <= col_id, values[:, :NRHS], 0.0)
+    shares_out[...] = shares[...]
+    basis[0] = jnp.dot(
+        values[:, NRHS:], remainder[...], precision=precise, preferred_element_type=jnp.float32
+    )
 
 
 def body(couplings, pivots, pattern, krylov):
@@ -323,39 +355,53 @@
     vmem = pl.BlockSpec(memory_space=pltpu.VMEM)
     hbm = pl.BlockSpec(memory_space=pl.ANY)
     dma = pltpu.SemaphoreType.DMA
-    return pl.pallas_call(
+    parts = NRHS // PART
+    remainder, shares, table = pl.pallas_call(
         functools.partial(kernel, blocks, ranks),
         out_shape=(
-            jax.ShapeDtypeStruct((1, NRHS, rows_here), jnp.float32),
-            jax.ShapeDtypeStruct((stored_count, NRHS), jnp.float32),
-            jax.ShapeDtypeStruct((NRHS, NRHS), jnp.float32),
+            jax.ShapeDtypeStruct((NRHS, rows_here), jnp.float32),
+            jax.ShapeDtypeStruct((NRHS, stored_count), jnp.float32),
+            jax.ShapeDtypeStruct((NRHS, 2 * NRHS), jnp.float32),
         ),
-        in_specs=[hbm, hbm, vmem, vmem],
+        in_specs=[hbm, hbm, hbm, hbm],
         out_specs=(vmem, vmem, vmem),
         scratch_shapes=[
+            pltpu.VMEM(pattern.shape, jnp.int32),
+            pltpu.VMEM(krylov.shape, jnp.float32),
             pltpu.VMEM((kinds, rows_here, width), jnp.bfloat16),
             pltpu.VMEM((rows_here, width), jnp.float32),
             pltpu.VMEM((rows_here, width), jnp.bfloat16),
             pltpu.VMEM((rows_here, width), jnp.bfloat16),
             pltpu.VMEM((kinds, fields, width), jnp.float32),
-            pltpu.VMEM((levels + 1, ranks, NRHS, rows_here), jnp.float32),
-            pltpu.VMEM((levels, 4, NRHS, rows_here), jnp.float32),
+            pltpu.VMEM((parts, levels + 1, ranks, PART, rows_here), jnp.float32),
+            pltpu.VMEM((parts, levels, 4, PART, rows_here), jnp.float32),
             pltpu.VMEM((2, ranks, SUBLANES, LANES), jnp.float32),
             pltpu.VMEM((2, blocks, SUBLANES, LANES), jnp.float32),
-            dma((kinds + 1,)),
-            dma((levels + 1, ranks)),
-            dma((levels + 1, ranks)),
-            dma((levels, 2)),
-            dma((levels, 2)),
+            dma((kinds + 3,)),
+            dma((parts, levels + 1, ranks)),
+            dma((parts, levels + 1, ranks)),
+            dma((parts, levels, 2)),
+            dma((parts, levels, 2)),
             dma((2, ranks)),
             dma((2, ranks)),
             dma((2, blocks)),
             dma((2, blocks)),
         ],
         compiler_params=pltpu.CompilerParams(
-            collective_id=0, has_side_effects=True, vmem_limit_bytes=48 * 1024 * 1024
+            collective_id=0, has_side_effects=True, vmem_limit_bytes=60 * 1024 * 1024
         ),
     )(couplings, pivots, pattern, krylov)
+    basis, shares, upper = pl.pallas_call(
+        finish,
+        out_shape=(
+            jax.ShapeDtypeStruct((1, NRHS, rows_here), jnp.float32),
+            jax.ShapeDtypeStruct((NRHS, stored_count), jnp.float32),
+            jax.ShapeDtypeStruct((NRHS, NRHS), jnp.float32),
+        ),
+        in_specs=[vmem, vmem, vmem],
+        out_specs=(vmem, vmem, vmem),
+    )(remainder, shares, table)
+    return basis, shares.T, upper
 
 
 def solution(mesh):

time: 51 us -> 47.6 us (0.933)
  local copies, waits for them, and re-layouts: 5.35 us -> 1.36 us
    unnamed x7 -> x1, local copies, waits for them, and re-layouts: 4.68 us -> 1.36 us
    pallas_call x0 -> x1, Pallas kernels: none -> 1.63 us  [body(): pl.pallas_call(finish, out_shape=(jax.ShapeDtypeStruct((1, NRHS, rows_her...]
    pallas_call x1, Pallas kernels: 44.8 us -> 43.7 us  [body(): pl.pallas_call(functools.partial(kernel, blocks, ranks), out_shape=(jax.S...]
    pallas_call x1 -> x0, local copies, waits for them, and re-layouts: 0.67 us -> none  [body(): pl.pallas_call(functools.partial(kernel, blocks, ranks), out_shape=(jax.S...]
where the time goes in v2:
time: 47.6 us; the launch traced here: 47.3 us
  Pallas kernels  45.3 us (95%)
  local copies, waits for them, and re-layouts  1.36 us (3%)
  between operations  0.64 us (1%)
    pallas_call x1, Pallas kernels, body(): pl.pallas_call(functools.partial(kernel, blocks, ranks), out_shape=(jax.S...  43.7 us
    pallas_call x1, Pallas kernels, body(): pl.pallas_call(finish, out_shape=(jax.ShapeDtypeStruct((1, NRHS, rows_her...  1.63 us
    unnamed x1, local copies, waits for them, and re-layouts  1.36 us

profile of v2, /device:TPU:0, one launch (start us, length us, event | category | flops | bytes accessed | tf_op | source)
XLA Modules:
  0.0 47.3 jit_solution(15171781913575108148)
XLA Ops:
  0.6 1.4 %copy.7.pattern_hbm = s32[1,6,9,9]{3,2,1,0:T(8,128)} copy(s32[1,6,9,9]{3,0,2,1:T(1,128)} %param.6) | data formatting | bytes 3888 | tf_op args[2]
  2.0 43.7 %shard_map.67 = (f32[16,432]{1,0:T(8,128)}, f32[16,32]{1,0:T(8,128)}, f32[16,32]{1,0:T(8,128)}) custom-call(bf16[1,6,432,1728]{3,2,1,0:T(8,128)(2,1)} %couplings.1, f32[1,432,1728]{2,1,0:T(8,128)} %pivots.1, s32[1,6,9,9]{3,2,1,0:T(8,128)} %copy.7.pattern_hbm, f32[1,32,432]{2,1,0:T(8,128)} %krylov_hbm.1), custom_call_target="tpu_custom_call" | custom-call | tf_op jit(solution)/shard_map/pallas_call | solution.py:359
  45.7 1.6 %shard_map.68 = (f32[1,16,432]{2,1,0:T(8,128)}, f32[16,32]{1,0:T(8,128)}, f32[16,16]{1,0:T(8,128)}) custom-call(f32[16,432]{1,0:T(8,128)} %get-tuple-element.9.remainder, f32[16,32]{1,0:T(8,128)} %get-tuple-element.10.shares, f32[16,32]{1,0:T(8,128)} %get-tuple-element.11.table), custom_call_target="tpu_custom_call" | custom-call | tf_op jit(solution)/shard_map/pallas_call | solution.py:394

commit v3 on v2

--- a/solution.py
+++ b/solution.py
@@ -96,7 +96,7 @@
     )
     for kind in range(kinds):
         keep[kind] = jnp.dot(
-            pattern[0, kind].astype(jnp.float32), col_onehot, preferred_element_type=jnp.float32
+            pattern[kind, :, 0, :].astype(jnp.float32), col_onehot, preferred_element_type=jnp.float32
         )
     pl.semaphore_wait(barrier, ranks + blocks - 2)
 
@@ -366,7 +366,7 @@
         in_specs=[hbm, hbm, hbm, hbm],
         out_specs=(vmem, vmem, vmem),
         scratch_shapes=[
-            pltpu.VMEM(pattern.shape, jnp.int32),
+            pltpu.VMEM((kinds, fields, 1, fields), jnp.int32),
             pltpu.VMEM(krylov.shape, jnp.float32),
             pltpu.VMEM((kinds, rows_here, width), jnp.bfloat16),
             pltpu.VMEM((rows_here, width), jnp.float32),
@@ -390,7 +390,7 @@
         compiler_params=pltpu.CompilerParams(
             collective_id=0, has_side_effects=True, vmem_limit_bytes=60 * 1024 * 1024
         ),
-    )(couplings, pivots, pattern, krylov)
+    )(couplings, pivots, pattern.transpose(1, 2, 0, 3), krylov)
     basis, shares, upper = pl.pallas_call(
         finish,
         out_shape=(

time: 47.6 us -> 46.6 us (0.979)
  local copies, waits for them, and re-layouts: 1.36 us -> 0 us
    unnamed x1 -> x0, local copies, waits for them, and re-layouts: 1.36 us -> none
where the time goes in v3:
time: 46.6 us; the launch traced here: 46.4 us
  Pallas kernels  45.7 us (98%)
  between operations  0.64 us (1%)
    pallas_call x1, Pallas kernels, body(): pl.pallas_call(functools.partial(kernel, blocks, ranks), out_shape=(jax.S...  44.1 us
    pallas_call x1, Pallas kernels, body(): pl.pallas_call(finish, out_shape=(jax.ShapeDtypeStruct((1, NRHS, rows_her...  1.63 us

profile of v3, /device:TPU:0, one launch (start us, length us, event | category | flops | bytes accessed | tf_op | source)
XLA Modules:
  0.0 46.4 jit_solution(13418423925878396944)
XLA Ops:
  0.6 44.1 %shard_map.67 = (f32[16,432]{1,0:T(8,128)}, f32[16,32]{1,0:T(8,128)}, f32[16,32]{1,0:T(8,128)}) custom-call(bf16[1,6,432,1728]{3,2,1,0:T(8,128)(2,1)} %couplings.1, f32[1,432,1728]{2,1,0:T(8,128)} %pivots.1, s32[6,9,1,9]{3,2,1,0:T(1,128)} %bitcast.2, f32[1,32,432]{2,1,0:T(8,128)} %krylov_hbm.1), custom_call_target="tpu_custom_call" | custom-call | tf_op jit(solution)/shard_map/pallas_call | solution.py:359
  44.7 1.6 %shard_map.68 = (f32[1,16,432]{2,1,0:T(8,128)}, f32[16,32]{1,0:T(8,128)}, f32[16,16]{1,0:T(8,128)}) custom-call(f32[16,432]{1,0:T(8,128)} %get-tuple-element.9.remainder, f32[16,32]{1,0:T(8,128)} %get-tuple-element.10.shares, f32[16,32]{1,0:T(8,128)} %get-tuple-element.11.table), custom_call_target="tpu_custom_call" | custom-call | tf_op jit(solution)/shard_map/pallas_call | solution.py:394
